TPU v7x, 256 devices: a whole 4x4x8 slice. The times are simulated.
256 devices in a mesh: blk: 32 (over z, x_hi, core), head: 8 (over y, x_lo).
Axes of the slice: x: 4 (x_hi: 2, x_lo: 2; x = x_hi * 2 + x_lo), y: 4, z: 8, core: 2. Of those that a mesh axis runs over, the one named last changes fastest.
Arguments:
- queries: bfloat16 [4096, 8192], P('blk', 'head'), may hold values from -6 to 6
- cached_prompt_keys: bfloat16 [16384, 1024], P('blk', 'head'), may hold values from -12 to 12
- cached_prompt_values: bfloat16 [16384, 1024], P('blk', 'head'), may hold values from -6 to 6
- rotated_response_keys: bfloat16 [4096, 1024], P('blk', 'head'), may hold values from -21 to 21
- packed_response_values: bfloat16 [4096, 1024], P('blk', 'head'), may hold values from -6 to 6
- segment_ids: int32 [4096], replicated, may hold values from 0 to 94, as said below
- out_weight: bfloat16 [8192, 8192], P('head', 'blk'), may hold values from -0.5 to 0.5
Outputs:
- attended: bfloat16 [4096, 8192], P('blk', 'head')
Inputs may be any that keep to these rules, and one draw needn't show every extreme that they name: `segment_ids`: starts at 0 and never falls along the rows, rising by at most one from row to row; every response has 1 to 128 consecutive rows, one exactly 128; a new response never begins at row k * 128 for k > 0. Each aligned run of 64 rows holds exactly one response start besides its first row, except the two runs that meet at row 128.
All inputs are finite; a program needn't handle non-finite values.
Results may differ from a plain program's by a relative error of at most 0.019.
Values may be sent and summed in bfloat16 or wider, within the bound.
A program may use at most 64 MiB of HBM per device.

v0:
```python
import math

import jax
import jax.numpy as jnp
from jax import lax
from jax.sharding import PartitionSpec as P

HEAD_WIDTH = 128


def shifted(block, axis, distance):
    devices = range(lax.axis_size(axis))
    route = [(i - distance, i) for i in devices if i - distance in devices]
    return lax.ppermute(block, axis, route)


def fold_keys(state_now, query_head_count, key_block, value_block, score_scale):
    row_top, row_total, weighted = state_now
    scores = (
        jnp.einsum(
            "rkgd,nkd->kgrn", query_head_count, key_block, preferred_element_type=jnp.float32
        )
        * score_scale
    )
    new_top = jnp.maximum(row_top, scores.max(axis=-1))
    shrink = jnp.exp(row_top - new_top)
    exp_scores = jnp.exp(scores - new_top[..., None])
    new_total = row_total * shrink + exp_scores.sum(axis=-1)
    update = jnp.einsum(
        "kgrn,nkd->kgrd",
        exp_scores.astype(jnp.bfloat16),
        value_block,
        preferred_element_type=jnp.float32,
    )
    return (new_top, new_total, weighted * shrink[..., None] + update)


def on_device(
    queries,
    cached_prompt_keys,
    cached_prompt_values,
    rotated_response_keys,
    packed_response_values,
    segment_ids,
    out_weight,
):
    row_count = queries.shape[0]
    heads_local = queries.shape[1] // HEAD_WIDTH
    kv_local = rotated_response_keys.shape[1] // HEAD_WIDTH
    group_width = heads_local // kv_local
    score_scale = 1.0 / math.sqrt(HEAD_WIDTH)
    query_head_count = queries.reshape(row_count, kv_local, group_width, HEAD_WIDTH)
    position = lax.axis_index("blk")
    before_keys, before_values = shifted((rotated_response_keys, packed_response_values), "blk", 1)
    near_keys = jnp.concatenate([before_keys, rotated_response_keys], axis=0).reshape(
        2 * row_count, kv_local, HEAD_WIDTH
    )
    near_values = jnp.concatenate([before_values, packed_response_values], axis=0).reshape(
        2 * row_count, kv_local, HEAD_WIDTH
    )
    own_start = position * row_count
    before_start = jnp.maximum(position - 1, 0) * row_count
    own_segments = lax.dynamic_slice_in_dim(segment_ids, own_start, row_count, 0)
    before_segments = lax.dynamic_slice_in_dim(segment_ids, before_start, row_count, 0)
    key_segments = jnp.concatenate([before_segments, own_segments], axis=0)
    local_rows = jnp.arange(row_count, dtype=jnp.int32)
    key_places = jnp.concatenate([local_rows - row_count, local_rows], axis=0)
    allowed = (key_segments[None, :] == own_segments[:, None]) & (
        key_places[None, :] <= local_rows[:, None]
    )
    allowed = allowed & ((key_places[None, :] >= 0) | (position > 0))
    near_scores = (
        jnp.einsum(
            "rkgd,nkd->kgrn", query_head_count, near_keys, preferred_element_type=jnp.float32
        )
        * score_scale
    )
    near_scores = jnp.where(allowed, near_scores, -1e30)
    row_top = near_scores.max(axis=-1)
    near_exp = jnp.where(allowed, jnp.exp(near_scores - row_top[..., None]), 0.0)
    row_total = near_exp.sum(axis=-1)
    weighted = jnp.einsum(
        "kgrn,nkd->kgrd",
        near_exp.astype(jnp.bfloat16),
        near_values,
        preferred_element_type=jnp.float32,
    )
    shard_piece = (
        lax.all_gather(cached_prompt_keys, "blk", axis=0, tiled=True),
        lax.all_gather(cached_prompt_values, "blk", axis=0, tiled=True),
    )
    key_count = shard_piece[0].shape[0]
    page_keys = shard_piece[0].reshape(key_count, kv_local, HEAD_WIDTH)
    page_values = shard_piece[1].reshape(key_count, kv_local, HEAD_WIDTH)
    key_tiles = page_keys.reshape(key_count // 512, 512, kv_local, HEAD_WIDTH)
    value_tiles = page_values.reshape(key_count // 512, 512, kv_local, HEAD_WIDTH)

    def one_tile(state_inner, tiles):
        return (fold_keys(state_inner, query_head_count, tiles[0], tiles[1], score_scale), None)

    state_out, unused = lax.scan(one_tile, (row_top, row_total, weighted), (key_tiles, value_tiles))
    row_top, row_total, weighted = state_out
    context = weighted / row_total[..., None]
    context = (
        jnp.transpose(context, (2, 0, 1, 3))
        .reshape(row_count, heads_local * HEAD_WIDTH)
        .astype(jnp.bfloat16)
    )
    partial_out = jnp.dot(
        context,
        lax.all_gather(out_weight, "blk", axis=1, tiled=True),
        preferred_element_type=jnp.float32,
    )
    result = lax.psum_scatter(
        partial_out.astype(jnp.bfloat16), "head", scatter_dimension=1, tiled=True
    )
    return result


def solution(mesh):
    return jax.shard_map(
        on_device,
        mesh=mesh,
        in_specs=(
            P("blk", "head"),
            P("blk", "head"),
            P("blk", "head"),
            P("blk", "head"),
            P("blk", "head"),
            P(),
            P("head", "blk"),
        ),
        out_specs=P("blk", "head"),
        check_vma=False,
    )
```

profile of v0, /device:TPU:16, one launch (start us, length us, event | category | flops | bytes accessed | tf_op | source)
XLA Modules:
  0.0 404.2 jit_solution(15939927227536425658)
XLA Ops:
  8.1 1.7 collective-permute-start
  9.8 5.2 %collective-permute-start.1 = (bf16[128,128]{1,0:T(8,128)(2,1)}, bf16[128,128]{1,0:T(8,128)(2,1)S(1)}, u32[]{:S(2)}, u32[]{:S(2)}) collective-permute-start(bf16[128,128]{1,0:T(8,128)(2,1)} %param.13), channel_id=1, source_target_pairs={{0,8},{8,16},{16,24},{24,32},{32,40},{40,48},{48,56},{56,64},{64,7... | collective-permute-start | bytes 98312 | tf_op jit(solution)/shard_map/ppermute | solution.py:14
  19.4 80.3 %all-gather.4.cloned.1.call-done = bf16[16384,128]{1,0:T(8,128)(2,1)} async-done(((bf16[512,128]{1,0:T(8,128)(2,1)}), bf16[16384,128]{1,0:T(8,128)(2,1)}) %all-gather.4.cloned.1.call-update) | async-done | bytes 4194320 | tf_op jit(solution)/shard_map/all_gather | solution.py:89
  99.8 86.3 %all-gather.6.cloned.1.call-done = bf16[16384,128]{1,0:T(8,128)(2,1)} async-done(((bf16[512,128]{1,0:T(8,128)(2,1)}), bf16[16384,128]{1,0:T(8,128)(2,1)}) %all-gather.6.cloned.1.call-update) | async-done | bytes 4194320 | tf_op jit(solution)/shard_map/all_gather | solution.py:90
  186.1 106.1 %while.14 = (s32[]{:T(128)}, f32[1,8,128]{2,1,0:T(8,128)S(1)}, f32[1,8,128]{2,1,0:T(8,128)S(1)}, f32[1,8,128,128]{3,2,1,0:T(8,128)S(1)}, bf16[32,512,1,128]{3,1,...) while((s32[]{:T(128)}, f32[1,8,128]{2,1,0:T(8,128)S(1)}, ...), condition=%wide.region_5.6_spmd, body=%wide.region_2.5_spmd.sunk | while | flops 272894976 | bytes 7930965 | solution.py:101
  187.4 1.5 fusion.52
  190.8 1.5 fusion.52
  194.1 1.5 fusion.52
  197.4 1.5 fusion.52
  200.7 1.5 fusion.52
  204.0 1.5 fusion.52
  207.3 1.5 fusion.52
  210.6 1.5 fusion.52
  213.9 1.5 fusion.52
  217.3 1.5 fusion.52
  220.6 1.5 fusion.52
  223.9 1.5 fusion.52
  227.2 1.5 fusion.52
  230.5 1.5 fusion.52
  233.8 1.5 fusion.52
  237.1 1.5 fusion.52
  240.4 1.5 fusion.52
  243.7 1.5 fusion.52
  247.0 1.6 fusion.52
  250.4 1.5 fusion.52
  253.7 1.5 fusion.52
  257.1 1.6 fusion.52
  260.4 1.5 fusion.52
  263.7 1.5 fusion.52
  292.4 45.7 %all-gather.8.cloned.1.call-done = bf16[1024,8192]{1,0:T(8,128)(2,1)} async-done(((bf16[1024,256]{1,0:T(8,128)(2,1)}), bf16[1024,8192]{1,0:T(8,128)(2,1)}) %all-gather.8.cloned.1.call-update) | async-done | bytes 16777232 | tf_op jit(solution)/shard_map/all_gather | solution.py:111
  338.1 9.6 %convolution_convert_fusion = bf16[128,8192]{1,0:T(8,128)(2,1)} fusion(bf16[128,1024]{0,1:T(8,128)(2,1)S(1)} %bitcast.109, bf16[1024,8192]{1,0:T(8,128)(2,1)} %all-gather.8.cloned.1.call-done), kind=kOutput, calls=%fused_computation.23 | convolution fusion | flops 2148532224 | bytes 19136512 | tf_op jit(solution)/shard_map/dot_general | solution.py:109
  347.7 50.0 %reduce-scatter.2.cloned.1.call-done = bf16[128,1024]{1,0:T(8,128)(2,1)} async-done(((bf16[128,8192]{1,0:T(8,128)(2,1)}), bf16[128,1024]{1,0:T(8,128)(2,1)}) %reduce-scatter.2.cloned.1.call-update) | async-done | bytes 262160 | tf_op jit(solution)/shard_map/reduce_scatter | solution.py:114
  (193 shorter events, 73.5 us)
Async XLA Ops:
  6.5 93.2 %all-gather.4.cloned.1.call-start = ((), (), s32[]{:S(2)}) async-start(), calls=%async_computation.1 | async-start | bytes 4325376 | tf_op jit(solution)/shard_map/all_gather | solution.py:89
  7.3 178.8 %all-gather.6.cloned.1.call-start = ((), (), s32[]{:S(2)}) async-start(), calls=%async_computation.2 | async-start | bytes 4325376 | tf_op jit(solution)/shard_map/all_gather | solution.py:90
  8.0 11.0 %copy-start = (bf16[128,128]{1,0:T(8,128)(2,1)S(1)}, bf16[128,128]{1,0:T(8,128)(2,1)}, u32[]{:S(2)}) copy-start(bf16[128,128]{1,0:T(8,128)(2,1)} %param.13) | copy-start | bytes 98308
  8.0 330.1 %all-gather.8.cloned.1.call-start = ((), (), s32[]{:S(2)}) async-start(), calls=%async_computation.3 | async-start | bytes 17301504 | tf_op jit(solution)/shard_map/all_gather | solution.py:111
  8.1 9.4 %collective-permute-start = (bf16[128,128]{1,0:T(8,128)(2,1)}, bf16[128,128]{1,0:T(8,128)(2,1)S(1)}, u32[]{:S(2)}, u32[]{:S(2)}) collective-permute-start(bf16[128,128]{1,0:T(8,128)(2,1)} %param.12), channel_id=1, source_target_pairs={{0,8},{8,16},{16,24},{24,32},{32,40},{40,48},{48,56},{56,64},{64,7... | collective-permute-start | bytes 98312 | tf_op jit(solution)/shard_map/ppermute | solution.py:14
  9.8 9.2 %collective-permute-start.1 = (bf16[128,128]{1,0:T(8,128)(2,1)}, bf16[128,128]{1,0:T(8,128)(2,1)S(1)}, u32[]{:S(2)}, u32[]{:S(2)}) collective-permute-start(bf16[128,128]{1,0:T(8,128)(2,1)} %param.13), channel_id=1, source_target_pairs={{0,8},{8,16},{16,24},{24,32},{32,40},{40,48},{48,56},{56,64},{64,7... | collective-permute-start | bytes 98312 | tf_op jit(solution)/shard_map/ppermute | solution.py:14
  15.1 382.7 %reduce-scatter.2.cloned.1.call-start = ((), (), s32[]{:S(2)}) async-start(), calls=%async_computation.4 | async-start | bytes 2359296 | tf_op jit(solution)/shard_map/reduce_scatter | solution.py:114
Sparse Core Ops, SparseCore 0:
  10.1 89.5 all-gather.3
  102.6 83.4 all-gather.5
  188.6 149.4 all-gather.7
  347.9 49.8 reduce-scatter.1
where the time goes:
time: 408 us; the launch traced here: 404 us
  waiting for transfers between devices  264 us (65%)
  matrix products  104 us (25%)
  between operations  13.3 us (3%)
  other arithmetic  12.3 us (3%)
  starting transfers between devices  7.07 us (2%)
    all_gather x1, waiting for transfers between devices, on_device(): lax.all_gather(cached_prompt_values, 'blk', axis=0, tiled=True)  86.3 us
    all_gather x1, waiting for transfers between devices, on_device(): lax.all_gather(cached_prompt_keys, 'blk', axis=0, tiled=True)  80.3 us
    reduce_scatter x1, waiting for transfers between devices, on_device(): lax.psum_scatter(partial_out.astype(jnp.bfloat16), 'head', scatter_dimens...  50 us
    dot_general x32, matrix products, fold_keys(): jnp.einsum('kgrn,nkd->kgrd', exp_scores.astype(jnp.bfloat16), value_block...  49 us
    all_gather x1, waiting for transfers between devices, on_device(): lax.all_gather(out_weight, 'blk', axis=1, tiled=True)  45.7 us
    dot_general x32, matrix products, fold_keys(): jnp.einsum('rkgd,nkd->kgrn', query_head_count, key_block, preferred_eleme...  43.3 us
    reduce_sum x32, other arithmetic, fold_keys(): new_total = row_total * shrink + exp_scores.sum(axis=-1)  11.3 us
    dot_general x1, matrix products, on_device(): jnp.dot(context, lax.all_gather(out_weight, 'blk', axis=1, tiled=True), p...  9.6 us
  transfers between devices with their start and end apart: 6, of which 4 were waited for; matrix products, arithmetic and copies ran while one was open for 27% of the time, Pallas kernels for 0%

commit v1 on v0

v1 whole, which is shorter than its diff:
```python
import functools
import math

import jax
import jax.numpy as jnp
from jax import lax
from jax.experimental import pallas as pl
from jax.experimental.pallas import tpu as pltpu
from jax.sharding import PartitionSpec as P

WIDTH = 128
ROWS = 128
GROUP = 8
KEYS = 512
HALF = GROUP * ROWS
SCALE = math.log2(math.e) / math.sqrt(WIDTH)
MESH = pl.DeviceIdType.MESH
F32 = jnp.float32
BF16 = jnp.bfloat16
VMEM = pl.BlockSpec(memory_space=pltpu.VMEM)


def place():
    b, h = lax.axis_index("blk"), lax.axis_index("head")
    return b, h, b // 4, (b // 2) % 2, b % 2


def remote(src, dst, send, recv, device):
    return pltpu.make_async_remote_copy(
        src_ref=src, dst_ref=dst, send_sem=send, recv_sem=recv, device_id=device, device_id_type=MESH
    )


def with_ones(v):
    return jnp.concatenate([v, jnp.ones_like(v)], axis=1)


def dot_t(a, b):
    return lax.dot_general(a, b, (((1,), (1,)), ((), ())), preferred_element_type=F32)


def both(x):
    return jnp.concatenate([x, x], axis=1)


def attention(
    q_ref, k_ref, v_ref, rk_ref, rv_ref, seg_ref, w_ref,
    ctx_ref, wg_ref,
    q_other, qs, kb, vb, nk, nv, top, acc, part_out, part_in, lse_out, lse_in,
    ring_send, core_send, kv_recv, near_send, near_recv, q_sem, w_send, w_recv, part_send, part_recv,
):
    b, h, z, xh, c = place()
    up, down = ((b + 4) % 32, h), ((b + 28) % 32, h)
    across, mate = (b + 2 - 4 * xh, h), (b + 1 - 2 * c, h)
    after, before = ((b + 1) % 32, h), ((b + 31) % 32, h)
    g = xh * 2 + c
    g_across = 2 - 2 * xh + c
    g_mate = xh * 2 + 1 - c

    barrier = pltpu.get_barrier_semaphore()
    for device in (up, down, across, mate, after, before):
        pl.semaphore_signal(barrier, inc=1, device_id=device, device_id_type=MESH)
    kb[z, c] = k_ref[...]
    vb[z, c] = v_ref[...]
    wg_ref[g] = w_ref[...]
    pl.semaphore_wait(barrier, 6)

    buffers = (kb, vb)

    def ring(which, direction, slot):
        buf = buffers[which].at[slot, c]
        return remote(buf, buf, ring_send.at[which, direction, slot], kv_recv.at[which, slot, c], (up, down)[direction])

    def to_mate(which, slot):
        buf = buffers[which].at[slot, c]
        return remote(buf, buf, core_send.at[which, slot], kv_recv.at[which, slot, c], mate)

    def landed(which, slot, core):
        buf = buffers[which].at[slot, core]
        pltpu.make_async_copy(buf, buf, kv_recv.at[which, slot, core]).wait()

    send_q = remote(q_ref, q_other, q_sem.at[0], q_sem.at[1], across)
    send_nk = remote(rk_ref, nk, near_send.at[0], near_recv.at[0], after)
    send_nv = remote(rv_ref, nv, near_send.at[1], near_recv.at[1], after)
    w_across = remote(wg_ref.at[g], wg_ref.at[g], w_send.at[0], w_recv.at[0], across)
    w_mate = remote(wg_ref.at[g], wg_ref.at[g], w_send.at[1], w_recv.at[1], mate)
    w_on = remote(wg_ref.at[g_across], wg_ref.at[g_across], w_send.at[2], w_recv.at[2], mate)
    send_part = remote(part_out, part_in, part_send.at[0], part_recv.at[0], across)
    send_lse = remote(lse_out, lse_in, part_send.at[1], part_recv.at[1], across)

    for which in (0, 1):
        for direction in (0, 1):
            ring(which, direction, z).start()
    send_q.start()
    send_nk.start()
    send_nv.start()
    for which in (0, 1):
        to_mate(which, z).start()

    for n in range(GROUP):
        qs[pl.ds(n * ROWS, ROWS), :] = q_ref[:, n * WIDTH : (n + 1) * WIDTH]
    other = pl.ds(HALF, HALF)
    top[other, :] = jnp.full((HALF, WIDTH), -1e30, F32)
    acc[other, :] = jnp.zeros((HALF, 2 * WIDTH), F32)

    own_ids = seg_ref[pl.ds(b, 1), :].astype(F32)
    before_ids = seg_ref[pl.ds(jnp.maximum(b - 1, 0), 1), :].astype(F32)
    row_ids = jnp.transpose(jnp.broadcast_to(own_ids, (ROWS, ROWS)))
    row = lax.broadcasted_iota(jnp.int32, (ROWS, ROWS), 0)
    column = lax.broadcasted_iota(jnp.int32, (ROWS, ROWS), 1)
    allow_own = (row_ids == jnp.broadcast_to(own_ids, (ROWS, ROWS))) & (column <= row)
    first = jnp.broadcast_to(b, (ROWS, ROWS)) > 0
    allow_before = (row_ids == jnp.broadcast_to(before_ids, (ROWS, ROWS))) & first
    bias = jnp.concatenate([jnp.where(allow_before, 1.0, 0.0), jnp.where(allow_own, 1.0, 0.0)], axis=1)
    allowed = bias > 0.5
    send_nk.wait_recv()
    send_nv.wait_recv()
    near_k = jnp.concatenate([nk[...], rk_ref[...]], axis=0)
    near_v = with_ones(jnp.concatenate([nv[...], rv_ref[...]], axis=0))
    for n in range(GROUP):
        rows = pl.ds(n * ROWS, ROWS)
        s = jnp.where(allowed, dot_t(qs[rows, :], near_k), -1e30)
        m = jnp.max(s, axis=1, keepdims=True) * SCALE
        p = jnp.where(allowed, jnp.exp2(s * SCALE - m), 0.0)
        acc[rows, :] = jnp.dot(p.astype(BF16), near_v, preferred_element_type=F32)
        top[rows, :] = jnp.broadcast_to(m, (ROWS, WIDTH))

    def tile(rows, keys, values):
        s = dot_t(qs[rows, :], keys)
        old = top[rows, :]
        new = jnp.maximum(old, jnp.max(s, axis=1, keepdims=True) * SCALE)
        shrink = jnp.exp2(old - new)
        p = jnp.exp2(s * SCALE - new[:, :1]).astype(BF16)
        acc[rows, :] = acc[rows, :] * both(shrink) + jnp.dot(p, values, preferred_element_type=F32)
        top[rows, :] = new

    def arrived(u):
        a, odd = (u + 1) // 2, u % 2
        slot = (z + a * (1 - 2 * odd) + 8) % 8
        landed(0, slot, c)
        landed(1, slot, c)
        to_mate(0, slot).start()
        to_mate(1, slot).start()

        @pl.when((odd == 1) & (a <= 3))
        def _():
            ring(0, 0, slot).start()

        @pl.when((odd == 1) & (a <= 2))
        def _():
            ring(1, 0, slot).start()

        @pl.when((odd == 0) & (a <= 2))
        def _():
            ring(0, 1, slot).start()

        @pl.when((odd == 0) & (a <= 3))
        def _():
            ring(1, 1, slot).start()

    eye = row == column

    def step(t, _):
        a, odd = (t + 1) // 2, t % 2
        slot = (z + a * (1 - 2 * odd) + 8) % 8
        landed(0, slot, 1 - c)
        landed(1, slot, 1 - c)

        def half(i, _):
            side = jnp.where(t == 0, i, 1 - i)

            @pl.when((t == 0) & (i == 1))
            def _():
                send_q.wait_recv()
                for n in range(GROUP):
                    qs[pl.ds(HALF + n * ROWS, ROWS), :] = q_other[:, n * WIDTH : (n + 1) * WIDTH]

            keys = kb[slot].reshape(2 * KEYS, WIDTH)
            values = with_ones(vb[slot].reshape(2 * KEYS, WIDTH))
            for n in range(GROUP):
                tile(pl.ds(pl.multiple_of(side * HALF + n * ROWS, ROWS), ROWS), keys, values)

            @pl.when((t == 7) & (i == 0))
            def _():
                for n in range(GROUP):
                    rows = pl.ds(HALF + n * ROWS, ROWS)
                    total = acc[rows, WIDTH:]
                    part_out[:, n * WIDTH : (n + 1) * WIDTH] = (acc[rows, :WIDTH] / total).astype(BF16)
                    lse = top[rows, :] + jnp.log2(total)
                    lse_out[pl.ds(n, 1), :] = jnp.sum(jnp.where(eye, lse, 0.0), axis=0, keepdims=True)
                send_part.start()
                send_lse.start()

            return 0

        lax.fori_loop(0, 2, half, 0)

        @pl.when((odd == 0) & (t < 6))
        def _():
            arrived(t + 1)
            arrived(t + 2)

        @pl.when(t == 6)
        def _():
            arrived(t + 1)
            w_across.wait_recv()
            w_on.start()

        @pl.when(t == 1)
        def _():
            w_across.start()
            w_mate.start()

        return 0

    lax.fori_loop(0, 8, step, 0)

    send_lse.wait_recv()
    send_part.wait_recv()
    for n in range(GROUP):
        rows = pl.ds(n * ROWS, ROWS)
        columns = slice(n * WIDTH, (n + 1) * WIDTH)
        total = acc[rows, WIDTH:]
        here = top[rows, :] + jnp.log2(total)
        there = jnp.transpose(jnp.broadcast_to(lse_in[pl.ds(n, 1), :], (ROWS, ROWS)))
        high = jnp.maximum(here, there)
        a, d = jnp.exp2(here - high), jnp.exp2(there - high)
        mixed = acc[rows, :WIDTH] * (a / total) + part_in[:, columns].astype(F32) * d
        ctx_ref[:, columns] = (mixed / (a + d)).astype(BF16)

    for which in (0, 1):
        ring(which, 0, z).wait_send()
        ring(which, 1, z).wait_send()
        for a in (1, 2, 3):
            if a <= 3 - which:
                ring(which, 0, (z + 8 - a) % 8).wait_send()
            if a <= 2 + which:
                ring(which, 1, (z + a) % 8).wait_send()
        for slot in range(8):
            to_mate(which, slot).wait_send()
    send_q.wait_send()
    send_nk.wait_send()
    send_nv.wait_send()
    send_part.wait_send()
    send_lse.wait_send()
    w_mate.wait()
    w_across.wait_send()
    w_on.wait()


def attend(q, k, v, rk, rv, seg, w):
    dma = pltpu.SemaphoreType.DMA
    return pl.pallas_call(
        attention,
        out_shape=(
            jax.ShapeDtypeStruct((ROWS, HALF), BF16),
            jax.ShapeDtypeStruct((4, 1024, 256), BF16),
        ),
        in_specs=[VMEM] * 7,
        out_specs=(VMEM, VMEM),
        scratch_shapes=[
            pltpu.VMEM((ROWS, HALF), BF16),
            pltpu.VMEM((2 * HALF, WIDTH), BF16),
            pltpu.VMEM((8, 2, KEYS, WIDTH), BF16),
            pltpu.VMEM((8, 2, KEYS, WIDTH), BF16),
            pltpu.VMEM((ROWS, WIDTH), BF16),
            pltpu.VMEM((ROWS, WIDTH), BF16),
            pltpu.VMEM((2 * HALF, WIDTH), F32),
            pltpu.VMEM((2 * HALF, 2 * WIDTH), F32),
            pltpu.VMEM((ROWS, HALF), BF16),
            pltpu.VMEM((ROWS, HALF), BF16),
            pltpu.VMEM((GROUP, ROWS), F32),
            pltpu.VMEM((GROUP, ROWS), F32),
            dma((2, 2, 8)),
            dma((2, 8)),
            dma((2, 8, 2)),
            dma((2,)),
            dma((2,)),
            dma((2,)),
            dma((3,)),
            dma((3,)),
            dma((2,)),
            dma((2,)),
        ],
        compiler_params=pltpu.CompilerParams(
            collective_id=0, has_side_effects=True, vmem_limit_bytes=48 * 2**20
        ),
    )(q, k, v, rk, rv, seg, w)


SUB = ROWS // 8


def projection(
    ctx_ref, w_ref, out_ref,
    cb, ps, pr, red, zr,
    ring_send, ring_recv, ps_send, ps_recv, z_send, z_recv, h_send, h_recv,
):
    b, h, z, xh, c = place()
    up, down = ((b + 4) % 32, h), ((b + 28) % 32, h)

    def at_z(n):
        return ((b + 4 * n) % 32, h)

    def at_h(n):
        return (b, (h + n) % 8)

    barrier = pltpu.get_barrier_semaphore()
    for n in range(1, 8):
        pl.semaphore_signal(barrier, inc=1, device_id=at_z(n), device_id_type=MESH)
        pl.semaphore_signal(barrier, inc=1, device_id=at_h(n), device_id_type=MESH)
    cb[z] = ctx_ref[...]
    pl.semaphore_wait(barrier, 14)

    def ring(part, direction, slot):
        buf = cb.at[slot, :, pl.ds(part * 512, 512)]
        return remote(buf, buf, ring_send.at[part, direction, slot], ring_recv.at[part, slot], (up, down)[direction])

    def landed(part, slot):
        buf = cb.at[slot, :, pl.ds(part * 512, 512)]
        pltpu.make_async_copy(buf, buf, ring_recv.at[part, slot]).wait()

    for part in (0, 1):
        for direction in (0, 1):
            ring(part, direction, z).start()

    def sub(n):
        return pl.ds(pl.multiple_of(n * SUB, SUB), SUB)

    def partial_to(slot, n):
        there = (h + n) % 8
        return remote(
            ps.at[slot, sub(there)], pr.at[slot, h], ps_send.at[slot, there], ps_recv.at[slot, h], (b, there)
        )

    def slot_of(t):
        a, odd = (t + 1) // 2, t % 2
        return (z + a * (1 - 2 * odd) + 8) % 8

    def arrived(u):
        a, odd = (u + 1) // 2, u % 2
        slot = slot_of(u)
        landed(0, slot)
        landed(1, slot)

        @pl.when((odd == 1) & (a <= 3))
        def _():
            ring(0, 0, slot).start()

        @pl.when((odd == 1) & (a <= 2))
        def _():
            ring(1, 0, slot).start()

        @pl.when((odd == 0) & (a <= 2))
        def _():
            ring(0, 1, slot).start()

        @pl.when((odd == 0) & (a <= 3))
        def _():
            ring(1, 1, slot).start()

    def step(t, _):
        slot = slot_of(t)

        @pl.when((t % 2 == 1) & (t < 7))
        def _():
            arrived(t)
            arrived(t + 1)

        @pl.when(t == 7)
        def _():
            arrived(t)

        rows = cb[slot]
        for part in range(4):
            ps[slot, :, part * 256 : (part + 1) * 256] = jnp.dot(
                rows, w_ref[part], preferred_element_type=F32
            ).astype(BF16)
        for n in range(1, 8):
            partial_to(slot, n).start()
        pr[slot, h] = ps[slot, sub(h), :]
        return 0

    lax.fori_loop(0, 8, step, 0)

    def to_z(slot):
        return remote(red.at[slot], zr.at[z], z_send.at[slot], z_recv.at[z], (slot * 4 + xh * 2 + c, h))

    def total(t, _):
        slot = slot_of(t)
        for n in range(1, 8):
            there = (h + n) % 8
            buf = pr.at[slot, there]
            pltpu.make_async_copy(buf, buf, ps_recv.at[slot, there]).wait()
        value = pr[slot, 0].astype(F32)
        for n in range(1, 8):
            value = value + pr[slot, n].astype(F32)
        red[slot] = value.astype(BF16)

        @pl.when(t == 0)
        def _():
            zr[z] = red[z]

        @pl.when(t > 0)
        def _():
            to_z(slot).start()

        return 0

    lax.fori_loop(0, 8, total, 0)

    def to_h(there):
        return remote(zr.at[there], out_ref.at[sub(h)], h_send.at[there], h_recv.at[h], (b, there))

    def last(t, _):
        slot = slot_of(t)

        @pl.when(t > 0)
        def _():
            buf = zr.at[slot]
            pltpu.make_async_copy(buf, buf, z_recv.at[slot]).wait()

        @pl.when(slot != h)
        def _():
            to_h(slot).start()

        @pl.when(slot == h)
        def _():
            out_ref[sub(h), :] = zr[h]

        return 0

    lax.fori_loop(0, 8, last, 0)

    for n in range(1, 8):
        there = (h + n) % 8
        buf = out_ref.at[sub(there)]
        pltpu.make_async_copy(buf, buf, h_recv.at[there]).wait()
    for n in range(1, 8):
        to_h((h + n) % 8).wait_send()
        to_z((z + n) % 8).wait_send()

    def sent(slot, _):
        for n in range(1, 8):
            partial_to(slot, n).wait_send()
        return 0

    lax.fori_loop(0, 8, sent, 0)
    for part in (0, 1):
        ring(part, 0, z).wait_send()
        ring(part, 1, z).wait_send()
        for a in (1, 2, 3):
            if a <= 3 - part:
                ring(part, 0, (z + 8 - a) % 8).wait_send()
            if a <= 2 + part:
                ring(part, 1, (z + a) % 8).wait_send()


def project(ctx, w):
    dma = pltpu.SemaphoreType.DMA
    return pl.pallas_call(
        projection,
        out_shape=jax.ShapeDtypeStruct((ROWS, 1024), BF16),
        in_specs=[VMEM] * 2,
        out_specs=VMEM,
        scratch_shapes=[
            pltpu.VMEM((8, ROWS, 1024), BF16),
            pltpu.VMEM((8, ROWS, 1024), BF16),
            pltpu.VMEM((8, 8, SUB, 1024), BF16),
            pltpu.VMEM((8, SUB, 1024), BF16),
            pltpu.VMEM((8, SUB, 1024), BF16),
            dma((2, 2, 8)),
            dma((2, 8)),
            dma((8, 8)),
            dma((8, 8)),
            dma((8,)),
            dma((8,)),
            dma((8,)),
            dma((8,)),
        ],
        compiler_params=pltpu.CompilerParams(
            collective_id=1, has_side_effects=True, vmem_limit_bytes=48 * 2**20
        ),
    )(ctx, w)


def on_device(q, k, v, rk, rv, seg, w):
    ctx, gathered = attend(q, k, v, rk, rv, seg.reshape(32, ROWS), w)
    return project(ctx, gathered)


def solution(mesh):
    return jax.shard_map(
        on_device,
        mesh=mesh,
        in_specs=(
            P("blk", "head"),
            P("blk", "head"),
            P("blk", "head"),
            P("blk", "head"),
            P("blk", "head"),
            P(),
            P("head", "blk"),
        ),
        out_specs=P("blk", "head"),
        check_vma=False,
    )
```

time: 408 us -> 113 us (0.28)
  waiting for transfers between devices: 264 us -> 0 us
  Pallas kernels: 0 us -> 106 us
  matrix products: 104 us -> 0 us
  between operations: 13.3 us -> 0.02 us
  other arithmetic: 12.3 us -> 0 us
  starting transfers between devices: 7.07 us -> 0 us
  local copies, waits for them, and re-layouts: 2.45 us -> 6.73 us
    all_gather x3 -> x0, waiting for transfers between devices: 212 us -> none  [the longest x1 86.3 us: on_device(): lax.all_gather(cached_prompt_values, 'blk', axis=0, tiled=True)]
    pallas_call x0 -> x2, Pallas kernels: none -> 106 us  [the longest x1 57.6 us: attend(): pl.pallas_call(attention, out_shape=(jax.ShapeDtypeStruct((ROWS, HALF), B...]
    dot_general x67 -> x0, matrix products: 104 us -> none  [the longest x32 49 us: fold_keys(): jnp.einsum('kgrn,nkd->kgrd', exp_scores.astype(jnp.bfloat16), value_block...]
    reduce_scatter x1 -> x0, waiting for transfers between devices: 50 us -> none  [on_device(): lax.psum_scatter(partial_out.astype(jnp.bfloat16), 'head', scatter_dimens...]
    reduce_sum x33 -> x0, other arithmetic: 11.5 us -> none  [the longest x32 11.3 us: fold_keys(): new_total = row_total * shrink + exp_scores.sum(axis=-1)]
    ppermute x2 -> x0, starting transfers between devices: 6.95 us -> none  [shifted(): return lax.ppermute(block, axis, route)]
    unnamed x3 -> x15, local copies, waits for them, and re-layouts: 1.13 us -> 6.73 us
  transfers between devices with their start and end apart: 6 -> 0, of which waited for: 4 -> 0; matrix products, arithmetic and copies ran while one was open for 27% -> 0% of each run, Pallas kernels for 0% -> 0%
where the time goes in v1:
time: 113 us
  Pallas kernels  106 us (94%)
  local copies, waits for them, and re-layouts  6.73 us (6%)
    pallas_call x1, Pallas kernels, attend(): pl.pallas_call(attention, out_shape=(jax.ShapeDtypeStruct((ROWS, HALF), B...  57.6 us
    pallas_call x1, Pallas kernels, project(): pl.pallas_call(projection, out_shape=jax.ShapeDtypeStruct((ROWS, 1024), B...  48.5 us
    unnamed x15, local copies, waits for them, and re-layouts  6.73 us

profile of v1, /device:TPU:16, one launch (start us, length us, event | category | flops | bytes accessed | tf_op | source)
XLA Modules:
  0.0 112.9 jit_solution(13211488231444952880)
XLA Ops:
  0.0 0.0 copy-start
  0.0 1.0 copy-done
  1.0 0.0 copy-start.1
  1.0 0.9 copy-done.1
  2.0 0.0 copy-start.2
  2.0 0.9 copy-done.2
  2.9 0.0 copy-start.3
  2.9 0.9 copy-done.3
  3.8 0.0 copy-start.4
  3.8 0.8 copy-done.4
  4.6 0.0 copy-start.5
  4.6 0.8 copy-done.5
  5.3 0.0 copy-start.6
  5.3 0.7 copy-done.6
  6.0 57.6 %shard_map.73 = (bf16[128,1024]{1,0:T(8,128)(2,1)S(1)}, bf16[4,1024,256]{2,1,0:T(8,128)(2,1)S(1)}) custom-call(bf16[128,1024]{1,0:T(8,128)(2,1)S(1)} %copy-done.1, bf16[512,128]{1,0:T(8,128)(2,1)S(1)} %copy-done.2, bf16[512,128]{1,0:T(8,128)(2,1)S(1)} %copy-done.3, bf16[128,128]{1,0:T(8,128)(2,1)S(1)} %copy-done.4, bf16[128,128]{1,0:T(8,128)(2,1)S(1)} %copy-done.5, ...), custom_call_target="tpu_custom_call" | custom-call | tf_op jit(solution)/shard_map/pallas_call | solution.py:253
  63.7 48.5 %shard_map.74 = bf16[128,1024]{1,0:T(8,128)(2,1)S(1)} custom-call(bf16[128,1024]{1,0:T(8,128)(2,1)S(1)} %get-tuple-element.7.ctx_ref, bf16[4,1024,256]{2,1,0:T(8,128)(2,1)S(1)} %get-tuple-element.8.w_ref), custom_call_target="tpu_custom_call" | custom-call | tf_op jit(solution)/shard_map/pallas_call | solution.py:461
  112.2 0.7 copy.9
Async XLA Ops:
  0.0 1.0 copy-start
  1.0 0.9 copy-start.1
  2.0 0.9 copy-start.2
  2.9 0.9 copy-start.3
  3.8 0.8 copy-start.4
  4.6 0.8 copy-start.5
  5.3 0.7 copy-start.6

commit v2 on v0

v2 whole, which is shorter than its diff:
```python
import functools
import math

import jax
import jax.numpy as jnp
from jax import lax
from jax.experimental import pallas as pl
from jax.experimental.pallas import tpu as pltpu
from jax.sharding import PartitionSpec as P

WIDTH = 128
ROWS = 128
GROUP = 8
PIECE = 256
SIDE = ROWS // 2
HALF = GROUP * ROWS
SCALE = math.log2(math.e) / math.sqrt(WIDTH)
MESH = pl.DeviceIdType.MESH
F32 = jnp.float32
BF16 = jnp.bfloat16
VMEM = pl.BlockSpec(memory_space=pltpu.VMEM)
ANY = pl.BlockSpec(memory_space=pl.ANY)


def place():
    b, h = lax.axis_index("blk"), lax.axis_index("head")
    return b, h, b // 4, (b // 2) % 2, b % 2


def remote(src, dst, send, recv, device):
    return pltpu.make_async_remote_copy(
        src_ref=src, dst_ref=dst, send_sem=send, recv_sem=recv, device_id=device, device_id_type=MESH
    )


def with_ones(v):
    return jnp.concatenate([v, jnp.ones_like(v)], axis=1)


def dot_t(a, b):
    return lax.dot_general(a, b, (((1,), (1,)), ((), ())), preferred_element_type=F32)


def both(x):
    return jnp.concatenate([x, x], axis=1)


def local(src, dst, sem):
    return pltpu.make_async_copy(src, dst, sem)


def waited(buf, sem):
    pltpu.make_async_copy(buf, buf, sem).wait()


def whole(
    q_hbm, k_hbm, v_hbm, rk_hbm, rv_hbm, seg_hbm, w_hbm,
    out_ref,
    q_ref, q_other, qs, qs_x, kv, near, seg_ref, top, top_x, acc, acc_x, part_out, part_in, lse_out, lse_in,
    wg, cb, half_sum, ps, pr, red, zr,
    load, ring_send, ring_recv, core_send, core_recv, near_send, near_recv, q_sem, w_send, w_recv,
    part_send, part_recv, lse_send, lse_recv, cb_send, cb_recv, ps_send, ps_recv, z_send, z_recv, h_send, h_recv,
):
    b, h, z, xh, c = place()
    up, down = ((b + 4) % 32, h), ((b + 28) % 32, h)
    across, mate = (b + 2 - 4 * xh, h), (b + 1 - 2 * c, h)
    after, before = ((b + 1) % 32, h), ((b + 31) % 32, h)
    g = xh * 2 + c
    y, xl = h // 2, h % 2
    beside, diagonal = (b, h + 1 - 2 * xl), (b + 2 - 4 * xh, h + 1 - 2 * xl)

    loads = [
        local(k_hbm.at[pl.ds(0, PIECE)], kv.at[0, 0, c, 0], load.at[0]),
        local(v_hbm.at[pl.ds(0, PIECE)], kv.at[0, 0, c, 1], load.at[1]),
        local(k_hbm.at[pl.ds(PIECE, PIECE)], kv.at[0, 1, c, 0], load.at[2]),
        local(v_hbm.at[pl.ds(PIECE, PIECE)], kv.at[0, 1, c, 1], load.at[3]),
        local(q_hbm, q_ref, load.at[4]),
        local(rk_hbm, near.at[0, 1], load.at[5]),
        local(rv_hbm, near.at[1, 1], load.at[6]),
        local(seg_hbm, seg_ref, load.at[7]),
        local(w_hbm, wg.at[0, g], load.at[8]),
    ]
    for copy in loads:
        copy.start()

    barrier = pltpu.get_barrier_semaphore()
    partners = [across, diagonal, mate, after, before]
    partners += [((b + 4 * n) % 32, h) for n in range(1, 8)] + [(b, (h + n) % 8) for n in range(1, 8)]
    for device in partners:
        pl.semaphore_signal(barrier, inc=1, device_id=device, device_id_type=MESH)
    pl.semaphore_wait(barrier, len(partners))

    def ring(buf, send, recv, u, d):
        def go(src):
            return remote(src, buf(u, d), send.at[u, d], recv.at[u, d], (up, down)[d])

        return go

    def kv_at(u, d):
        return kv.at[u, d, c]

    def cb_at(u, d):
        return cb.at[u, d]

    def pass_on(at, send, recv, u):
        for d in (0, 1):
            waited(at(u, d), recv.at[u, d])

            @pl.when(u <= 4)
            def _():
                ring(at, send, recv, u + 2, d)(at(u, d)).start()

            @pl.when(u == 5 + d)
            def _():
                ring(at, send, recv, 7, d)(at(u, d)).start()

    def begin(at, send, recv, piece):
        for d in (0, 1):
            ring(at, send, recv, 1 + piece, d)(at(0, piece)).start()

    def all_sent(at, send, recv):
        for u in range(1, 8):
            for d in (0, 1):
                ring(at, send, recv, u, d)(at(u, d)).wait_send()

    def to_mate(u, d):
        return remote(kv_at(u, d), kv_at(u, d), core_send.at[u, d], core_recv.at[u, d], mate)

    send_q = remote(q_hbm, q_other, q_sem.at[0], q_sem.at[1], across)
    send_nk = remote(rk_hbm, near.at[0, 0], near_send.at[0], near_recv.at[0], after)
    send_nv = remote(rv_hbm, near.at[1, 0], near_send.at[1], near_recv.at[1], after)
    def spread_w(k):
        source, dest = wg.at[0, g], wg.at[(0, 1, 1)[k], g]
        return remote(source, dest, w_send.at[k], w_recv.at[k], (across, diagonal, beside)[k])

    g_across = 2 - 2 * xh + c

    def mate_w(k):
        buf = wg.at[(0, 1, 1, 0)[k], (g_across, g_across, g, g)[k]]
        return remote(buf, buf, w_send.at[3 + k], w_recv.at[3 + k], mate)

    def send_part(part):
        return remote(
            part_out.at[part], part_in.at[part], part_send.at[part], part_recv.at[part], (across, diagonal, beside)[part]
        )

    def send_lse(part):
        return remote(
            lse_out.at[part], lse_in.at[part], lse_send.at[part], lse_recv.at[part], (across, diagonal, beside)[part]
        )

    send_q.start()
    send_nk.start()
    send_nv.start()
    loads[0].wait()
    loads[1].wait()
    begin(kv_at, ring_send, ring_recv, 0)
    loads[2].wait()
    loads[3].wait()
    begin(kv_at, ring_send, ring_recv, 1)
    to_mate(0, 0).start()
    to_mate(0, 1).start()
    for copy in loads[4:]:
        copy.wait()

    for n in range(GROUP):
        for p in (0, 1):
            qs[pl.ds(p * 512 + n * SIDE, SIDE), :] = q_ref[p * SIDE : (p + 1) * SIDE, n * WIDTH : (n + 1) * WIDTH]
    top_x[...] = jnp.full((HALF, WIDTH), -1e30, F32)
    acc_x[...] = jnp.zeros((HALF, 2 * WIDTH), F32)

    own_ids = seg_ref[pl.ds(b, 1), :].astype(F32)
    before_ids = seg_ref[pl.ds(jnp.maximum(b - 1, 0), 1), :].astype(F32)
    row_ids = jnp.transpose(jnp.broadcast_to(own_ids, (ROWS, ROWS)))
    row = lax.broadcasted_iota(jnp.int32, (ROWS, ROWS), 0)
    column = lax.broadcasted_iota(jnp.int32, (ROWS, ROWS), 1)
    allow_own = (row_ids == jnp.broadcast_to(own_ids, (ROWS, ROWS))) & (column <= row)
    first = jnp.broadcast_to(b, (ROWS, ROWS)) > 0
    allow_before = (row_ids == jnp.broadcast_to(before_ids, (ROWS, ROWS))) & first
    allowed = jnp.concatenate([jnp.where(allow_before, 1.0, 0.0), jnp.where(allow_own, 1.0, 0.0)], axis=1)
    allowed = [jnp.concatenate([allowed[p * SIDE : (p + 1) * SIDE]] * 2, axis=0) > 0.5 for p in (0, 1)]
    send_nk.wait_recv()
    send_nv.wait_recv()
    near_k = near[0].reshape(2 * ROWS, WIDTH)
    near_v = with_ones(near[1].reshape(2 * ROWS, WIDTH))
    for n in range(GROUP):
        rows = pl.ds(n * ROWS, ROWS)
        s = jnp.where(allowed[n // 4], dot_t(qs[rows, :], near_k), -1e30)
        m = jnp.max(s, axis=1, keepdims=True) * SCALE
        p = jnp.where(allowed[n // 4], jnp.exp2(s * SCALE - m), 0.0)
        acc[rows, :] = jnp.dot(p.astype(BF16), near_v, preferred_element_type=F32)
        top[rows, :] = jnp.broadcast_to(m, (ROWS, WIDTH))

    own, partner = (qs, top, acc), (qs_x, top_x, acc_x)

    def tile(refs, n, keys, values):
        q, t, total = refs
        rows = pl.ds(n, ROWS) if isinstance(n, int) else pl.ds(pl.multiple_of(n, ROWS), ROWS)
        s = dot_t(q[rows, :], keys)
        old = t[rows, :]
        new = jnp.maximum(old, jnp.max(s, axis=1, keepdims=True) * SCALE)
        shrink = jnp.exp2(old - new)
        p = jnp.exp2(s * SCALE - new[:, :1]).astype(BF16)
        total[rows, :] = total[rows, :] * both(shrink) + jnp.dot(p, values, preferred_element_type=F32)
        t[rows, :] = new

    eye = row == column

    def unit(u):
        keys = kv[u, :, :, 0].reshape(4 * PIECE, WIDTH)
        return keys, with_ones(kv[u, :, :, 1].reshape(4 * PIECE, WIDTH))

    def step(t, _):
        new = (t <= 1) | ((t >= 4) & (t <= 8)) | (t == 10)
        u = jnp.where(t <= 1, t, jnp.where(t <= 3, t - 2, jnp.where(t <= 8, t - 2, jnp.where(t == 9, 6, 7))))

        @pl.when(new)
        def _():
            for d in (0, 1):
                waited(kv.at[u, d, 1 - c], core_recv.at[u, d])

        @pl.when(t == 2)
        def _():
            send_q.wait_recv()
            for n in range(GROUP):
                for p in (0, 1):
                    x = q_other[p * SIDE : (p + 1) * SIDE, n * WIDTH : (n + 1) * WIDTH]
                    qs_x[pl.ds(p * 512 + n * SIDE, SIDE), :] = x

        @pl.when((t <= 1) | (t == 9))
        def _():
            keys, values = unit(u)
            for n in range(GROUP):
                tile(own, n * ROWS, keys, values)

        @pl.when((t == 2) | (t == 3) | (t == 8))
        def _():
            keys, values = unit(u)
            for n in range(GROUP):
                tile(partner, n * ROWS, keys, values)

        @pl.when((t >= 4) & (t <= 7))
        def _():
            keys, values = unit(u)
            for n in range(GROUP):
                tile(partner, n * ROWS, keys, values)
                tile(own, n * ROWS, keys, values)

        @pl.when(t == 10)
        def _():
            keys, values = unit(u)
            for part in (0, 1, 2):
                refs = (partner, partner, own)[part]
                base = xl * 512 if part == 0 else (1 - xl) * 512
                for n in range(4):
                    tile(refs, base + n * ROWS, keys, values)
                for n in range(4):
                    rows = pl.ds(pl.multiple_of(base + n * ROWS, ROWS), ROWS)
                    total = refs[2][rows, WIDTH:]
                    part_out[part, pl.ds(n * ROWS, ROWS), :] = (refs[2][rows, :WIDTH] / total).astype(BF16)
                    lse = refs[1][rows, :] + jnp.log2(total)
                    lse_out[part, pl.ds(n, 1), :] = jnp.sum(jnp.where(eye, lse, 0.0), axis=0, keepdims=True)
                send_part(part).start()
                send_lse(part).start()
            for n in range(4):
                tile(own, xl * 512 + n * ROWS, keys, values)

        @pl.when((t <= 1) | ((t >= 3) & (t <= 6)) | (t == 8))
        def _():
            after_it = jnp.where(t <= 1, t + 1, jnp.where(t == 8, 7, t))
            pass_on(kv_at, ring_send, ring_recv, after_it)
            to_mate(after_it, 0).start()
            to_mate(after_it, 1).start()

        @pl.when(t == 0)
        def _():
            for k in (2, 1, 0):
                spread_w(k).start()
            mate_w(3).start()

        @pl.when(t == 6)
        def _():
            for k in (1, 2):
                spread_w(k).wait_recv()
                mate_w(k).start()

        @pl.when(t == 9)
        def _():
            spread_w(0).wait_recv()
            mate_w(0).start()

        return 0

    lax.fori_loop(0, 11, step, 0)

    def column(part, n):
        return jnp.transpose(jnp.broadcast_to(lse_in[part, pl.ds(n, 1), :], (ROWS, ROWS)))

    def mix(piece, n, o, lse, part):
        there = column(part, n)
        high = jnp.maximum(lse, there)
        a, d = jnp.exp2(lse - high), jnp.exp2(there - high)
        mixed = o * a + part_in[part, pl.ds(n * ROWS, ROWS), :].astype(F32) * d
        mixed = (mixed / (a + d)).astype(BF16)
        cb[0, piece, :, 2 * n * WIDTH : (2 * n + 1) * WIDTH] = mixed[:SIDE]
        cb[0, piece, :, (2 * n + 1) * WIDTH : (2 * n + 2) * WIDTH] = mixed[SIDE:]

    def received(part):
        send_part(part).wait_recv()
        send_lse(part).wait_recv()

    received(0)
    for n in range(4):
        rows = pl.ds(pl.multiple_of(xl * 512 + n * ROWS, ROWS), ROWS)
        total = acc[rows, WIDTH:]
        mix(0, n, acc[rows, :WIDTH] / total, top[rows, :] + jnp.log2(total), 0)
    begin(cb_at, cb_send, cb_recv, 0)
    received(1)
    received(2)
    for n in range(4):
        mix(1, n, part_in[1, pl.ds(n * ROWS, ROWS), :].astype(F32), column(1, n), 2)
    begin(cb_at, cb_send, cb_recv, 1)

    for k in range(4):
        mate_w(k).wait_recv()

    def partial_to(k, there):
        return remote(ps.at[k, there], pr.at[k, y], ps_send.at[k, there], ps_recv.at[k, y], (b, there * 2 + xl))

    def each_y(act):
        for n in range(1, 4):
            act((y + n) % 4)

    def spread(k):
        each_y(lambda there: partial_to(k, there).start())

    def alone(k, u):
        for q in range(4):
            value = jnp.dot(cb[u, 0], wg[0, q], preferred_element_type=F32)
            value = value + jnp.dot(cb[u, 1], wg[1, q], preferred_element_type=F32)
            ps[k, q, 0] = value.astype(BF16)
            ps[k, q, 1] = jnp.zeros((SIDE, 256), BF16)
        spread(k)

    def to_z(k, d):
        there = (z + k * (2 * d - 1) + 8) % 8
        return remote(red.at[k, d], zr.at[z], z_send.at[k, d], z_recv.at[z], (there * 4 + g, h))

    def sum_up(k):
        each_y(lambda there: waited(pr.at[k, there], ps_recv.at[k, there]))
        value = ps[k, y].astype(F32)
        for n in range(1, 4):
            value = value + pr[k, (y + n) % 4].astype(F32)
        red[k] = value.astype(BF16)

        @pl.when(k > 0)
        def _():
            to_z(k, 0).start()

        @pl.when((k > 0) & (k < 4))
        def _():
            to_z(k, 1).start()

    def out_at(row_half, block):
        rows = pl.ds(pl.multiple_of(row_half * SIDE, SIDE), SIDE)
        return out_ref.at[rows, pl.ds(pl.multiple_of(block * 256, 256), 256)]

    def to_h(buf, there):
        return remote(buf, out_at(xl, y), h_send.at[there], h_recv.at[h], (b, there))

    def hand_over(buf, source):
        @pl.when(source != h)
        def _():
            to_h(buf, source).start()

        @pl.when(source == h)
        def _():
            out_at(xl, y)[...] = buf[...]

    def deliver(k, d):
        source = (z + k * (1 - 2 * d) + 8) % 8
        waited(zr.at[source], z_recv.at[source])
        hand_over(zr.at[source], source)

    alone(0, 0)

    def stage(k, _):
        u = 2 * k - 1
        pass_on(cb_at, cb_send, cb_recv, u)
        rows = cb[u].reshape(ROWS, 1024)
        for q in range(4):
            half_sum[q] = jnp.dot(rows, wg[0, q], preferred_element_type=F32)
        pass_on(cb_at, cb_send, cb_recv, u + 1)
        rows = cb[u + 1].reshape(ROWS, 1024)
        for q in range(4):
            value = (half_sum[q] + jnp.dot(rows, wg[1, q], preferred_element_type=F32)).astype(BF16)
            ps[k, q] = value.reshape(2, SIDE, 256)
        spread(k)

        @pl.when(k >= 2)
        def _():
            sum_up(k - 1)

        @pl.when(k == 3)
        def _():
            deliver(1, 0)
            deliver(1, 1)

        return 0

    lax.fori_loop(1, 4, stage, 0)
    sum_up(0)
    hand_over(red.at[0, 0], z)
    pass_on(cb_at, cb_send, cb_recv, 7)
    alone(4, 7)
    sum_up(3)
    deliver(2, 0)
    deliver(2, 1)
    sum_up(4)
    deliver(3, 0)
    deliver(3, 1)
    deliver(4, 0)

    for n in range(1, 8):
        source = (h + n) % 8
        waited(out_at(source % 2, source // 2), h_recv.at[source])

    for n in range(8):
        source = (z + n) % 8

        @pl.when(source != h)
        def _():
            to_h(zr.at[source], source).wait_send()

    for k in range(5):
        each_y(lambda there: partial_to(k, there).wait_send())
        if k > 0:
            to_z(k, 0).wait_send()
        if 0 < k < 4:
            to_z(k, 1).wait_send()
    all_sent(cb_at, cb_send, cb_recv)
    all_sent(kv_at, ring_send, ring_recv)
    for u in range(8):
        for d in (0, 1):
            to_mate(u, d).wait_send()
    send_q.wait_send()
    send_nk.wait_send()
    send_nv.wait_send()
    for k in range(3):
        send_part(k).wait_send()
        send_lse(k).wait_send()
        spread_w(k).wait_send()
    for k in range(4):
        mate_w(k).wait_send()


def on_device(q, k, v, rk, rv, seg, w):
    dma = pltpu.SemaphoreType.DMA
    return pl.pallas_call(
        whole,
        out_shape=jax.ShapeDtypeStruct((ROWS, 1024), BF16),
        in_specs=[ANY] * 7,
        out_specs=VMEM,
        scratch_shapes=[
            pltpu.VMEM((ROWS, HALF), BF16),
            pltpu.VMEM((ROWS, HALF), BF16),
            pltpu.VMEM((HALF, WIDTH), BF16),
            pltpu.VMEM((HALF, WIDTH), BF16),
            pltpu.VMEM((8, 2, 2, 2, PIECE, WIDTH), BF16),
            pltpu.VMEM((2, 2, ROWS, WIDTH), BF16),
            pltpu.VMEM((32, ROWS), jnp.int32),
            pltpu.VMEM((HALF, WIDTH), F32),
            pltpu.VMEM((HALF, WIDTH), F32),
            pltpu.VMEM((HALF, 2 * WIDTH), F32),
            pltpu.VMEM((HALF, 2 * WIDTH), F32),
            pltpu.VMEM((3, 4 * ROWS, WIDTH), BF16),
            pltpu.VMEM((3, 4 * ROWS, WIDTH), BF16),
            pltpu.VMEM((3, 4, ROWS), F32),
            pltpu.VMEM((3, 4, ROWS), F32),
            pltpu.VMEM((2, 4, 1024, 256), BF16),
            pltpu.VMEM((8, 2, SIDE, 1024), BF16),
            pltpu.VMEM((4, ROWS, 256), F32),
            pltpu.VMEM((5, 4, 2, SIDE, 256), BF16),
            pltpu.VMEM((5, 4, 2, SIDE, 256), BF16),
            pltpu.VMEM((5, 2, SIDE, 256), BF16),
            pltpu.VMEM((8, SIDE, 256), BF16),
            dma((9,)),
            dma((8, 2)), dma((8, 2)),
            dma((8, 2)), dma((8, 2)),
            dma((2,)), dma((2,)),
            dma((2,)),
            dma((7,)), dma((7,)),
            dma((3,)), dma((3,)),
            dma((3,)), dma((3,)),
            dma((8, 2)), dma((8, 2)),
            dma((5, 4)), dma((5, 4)),
            dma((5, 2)), dma((8,)),
            dma((8,)), dma((8,)),
        ],
        compiler_params=pltpu.CompilerParams(
            collective_id=0, has_side_effects=True, vmem_limit_bytes=56 * 2**20
        ),
    )(q, k, v, rk, rv, seg.reshape(32, ROWS), w)


def solution(mesh):
    return jax.shard_map(
        on_device,
        mesh=mesh,
        in_specs=(
            P("blk", "head"),
            P("blk", "head"),
            P("blk", "head"),
            P("blk", "head"),
            P("blk", "head"),
            P(),
            P("head", "blk"),
        ),
        out_specs=P("blk", "head"),
        check_vma=False,
    )
```

time: 408 us -> 93.6 us (0.23)
  waiting for transfers between devices: 264 us -> 0 us
  matrix products: 104 us -> 0 us
  Pallas kernels: 0 us -> 91 us
  between operations: 13.3 us -> 0.01 us
  other arithmetic: 12.3 us -> 0 us
  starting transfers between devices: 7.07 us -> 0 us
    all_gather x3 -> x0, waiting for transfers between devices: 212 us -> none  [the longest x1 86.3 us: on_device(): lax.all_gather(cached_prompt_values, 'blk', axis=0, tiled=True)]
    dot_general x67 -> x0, matrix products: 104 us -> none  [the longest x32 49 us: fold_keys(): jnp.einsum('kgrn,nkd->kgrd', exp_scores.astype(jnp.bfloat16), value_block...]
    pallas_call x0 -> x1, Pallas kernels: none -> 91 us  [on_device(): pl.pallas_call(whole, out_shape=jax.ShapeDtypeStruct((ROWS, 1024), BF16),...]
    reduce_scatter x1 -> x0, waiting for transfers between devices: 50 us -> none  [on_device(): lax.psum_scatter(partial_out.astype(jnp.bfloat16), 'head', scatter_dimens...]
    reduce_sum x33 -> x0, other arithmetic: 11.5 us -> none  [the longest x32 11.3 us: fold_keys(): new_total = row_total * shrink + exp_scores.sum(axis=-1)]
    ppermute x2 -> x0, starting transfers between devices: 6.95 us -> none  [shifted(): return lax.ppermute(block, axis, route)]
  transfers between devices with their start and end apart: 6 -> 0, of which waited for: 4 -> 0; matrix products, arithmetic and copies ran while one was open for 27% -> 0% of each run, Pallas kernels for 0% -> 0%
where the time goes in v2:
time: 93.6 us; the launch traced here: 92.7 us
  Pallas kernels  91 us (97%)
  local copies, waits for them, and re-layouts  1.67 us (2%)
    pallas_call x1, Pallas kernels, on_device(): pl.pallas_call(whole, out_shape=jax.ShapeDtypeStruct((ROWS, 1024), BF16),...  91 us

profile of v2, /device:TPU:16, one launch (start us, length us, event | category | flops | bytes accessed | tf_op | source)
XLA Modules:
  0.0 92.7 jit_solution(13414336353221208915)
XLA Ops:
  0.0 91.0 %shard_map.73 = bf16[128,1024]{1,0:T(8,128)(2,1)} custom-call(bf16[128,1024]{1,0:T(8,128)(2,1)} %q_hbm.1, bf16[512,128]{1,0:T(8,128)(2,1)} %k_hbm.1, bf16[512,128]{1,0:T(8,128)(2,1)} %v_hbm.1, bf16[128,128]{1,0:T(8,128)(2,1)} %rk_hbm.1, bf16[128,128]{1,0:T(8,128)(2,1)} %rv_hbm.1, s32[32,128]{1,0:T(8,128)} %bitcast.1, bf16[1024,256]{1,0:T(8,128)(2,1)} %w_hbm.1), custom_call_target="tpu_custom_call" | custom-call | tf_op jit(solution)/shard_map/pallas_call | solution.py:459
  91.0 1.7 %copy.9 = bf16[128,1024]{1,0:T(8,128)(2,1)} copy(bf16[128,1024]{1,0:T(8,128)(2,1)} %shard_map.73) | data formatting | bytes 524288

commit v3 on v2

--- a/solution.py
+++ b/solution.py
@@ -139,9 +139,11 @@
         buf = wg.at[(0, 1, 1, 0)[k], (g_across, g_across, g, g)[k]]
         return remote(buf, buf, w_send.at[3 + k], w_recv.at[3 + k], mate)
 
-    def send_part(part):
+    def send_part(part, s):
+        rows = pl.ds(s * 2 * ROWS, 2 * ROWS)
+        device = (across, diagonal, beside)[part]
         return remote(
-            part_out.at[part], part_in.at[part], part_send.at[part], part_recv.at[part], (across, diagonal, beside)[part]
+            part_out.at[part, rows], part_in.at[part, rows], part_send.at[part, s], part_recv.at[part, s], device
         )
 
     def send_lse(part):
@@ -166,8 +168,9 @@
     for n in range(GROUP):
         for p in (0, 1):
             qs[pl.ds(p * 512 + n * SIDE, SIDE), :] = q_ref[p * SIDE : (p + 1) * SIDE, n * WIDTH : (n + 1) * WIDTH]
-    top_x[...] = jnp.full((HALF, WIDTH), -1e30, F32)
-    acc_x[...] = jnp.zeros((HALF, 2 * WIDTH), F32)
+    for t_ref, a_ref in ((top, acc), (top_x, acc_x)):
+        t_ref[...] = jnp.full((HALF, WIDTH), -1e30, F32)
+        a_ref[...] = jnp.zeros((HALF, 2 * WIDTH), F32)
 
     own_ids = seg_ref[pl.ds(b, 1), :].astype(F32)
     before_ids = seg_ref[pl.ds(jnp.maximum(b - 1, 0), 1), :].astype(F32)
@@ -179,29 +182,21 @@
     allow_before = (row_ids == jnp.broadcast_to(before_ids, (ROWS, ROWS))) & first
     allowed = jnp.concatenate([jnp.where(allow_before, 1.0, 0.0), jnp.where(allow_own, 1.0, 0.0)], axis=1)
     allowed = [jnp.concatenate([allowed[p * SIDE : (p + 1) * SIDE]] * 2, axis=0) > 0.5 for p in (0, 1)]
-    send_nk.wait_recv()
-    send_nv.wait_recv()
-    near_k = near[0].reshape(2 * ROWS, WIDTH)
-    near_v = with_ones(near[1].reshape(2 * ROWS, WIDTH))
-    for n in range(GROUP):
-        rows = pl.ds(n * ROWS, ROWS)
-        s = jnp.where(allowed[n // 4], dot_t(qs[rows, :], near_k), -1e30)
-        m = jnp.max(s, axis=1, keepdims=True) * SCALE
-        p = jnp.where(allowed[n // 4], jnp.exp2(s * SCALE - m), 0.0)
-        acc[rows, :] = jnp.dot(p.astype(BF16), near_v, preferred_element_type=F32)
-        top[rows, :] = jnp.broadcast_to(m, (ROWS, WIDTH))
-
     own, partner = (qs, top, acc), (qs_x, top_x, acc_x)
 
-    def tile(refs, n, keys, values):
+    def tile(refs, n, keys, values, allow=None):
         q, t, total = refs
         rows = pl.ds(n, ROWS) if isinstance(n, int) else pl.ds(pl.multiple_of(n, ROWS), ROWS)
         s = dot_t(q[rows, :], keys)
+        if allow is not None:
+            s = jnp.where(allow, s, -1e30)
         old = t[rows, :]
         new = jnp.maximum(old, jnp.max(s, axis=1, keepdims=True) * SCALE)
         shrink = jnp.exp2(old - new)
-        p = jnp.exp2(s * SCALE - new[:, :1]).astype(BF16)
-        total[rows, :] = total[rows, :] * both(shrink) + jnp.dot(p, values, preferred_element_type=F32)
+        p = jnp.exp2(s * SCALE - new[:, :1])
+        if allow is not None:
+            p = jnp.where(allow, p, 0.0)
+        total[rows, :] = total[rows, :] * both(shrink) + jnp.dot(p.astype(BF16), values, preferred_element_type=F32)
         t[rows, :] = new
 
     eye = row == column
@@ -210,36 +205,44 @@
         keys = kv[u, :, :, 0].reshape(4 * PIECE, WIDTH)
         return keys, with_ones(kv[u, :, :, 1].reshape(4 * PIECE, WIDTH))
 
+    def from_mate(u):
+        for d in (0, 1):
+            waited(kv.at[u, d, 1 - c], core_recv.at[u, d])
+
+    def receive(u):
+        pass_on(kv_at, ring_send, ring_recv, u)
+        to_mate(u, 0).start()
+        to_mate(u, 1).start()
+
     def step(t, _):
-        new = (t <= 1) | ((t >= 4) & (t <= 8)) | (t == 10)
-        u = jnp.where(t <= 1, t, jnp.where(t <= 3, t - 2, jnp.where(t <= 8, t - 2, jnp.where(t == 9, 6, 7))))
-
-        @pl.when(new)
-        def _():
-            for d in (0, 1):
-                waited(kv.at[u, d, 1 - c], core_recv.at[u, d])
-
-        @pl.when(t == 2)
-        def _():
-            send_q.wait_recv()
+        u = jnp.where(t <= 1, 0, jnp.where(t <= 2, 1, t - 3))
+
+        @pl.when((t == 0) | (t == 2) | (t >= 5))
+        def _():
+            from_mate(u)
+
+        @pl.when(t == 1)
+        def _():
+            send_nk.wait_recv()
+            send_nv.wait_recv()
+            near_k = near[0].reshape(2 * ROWS, WIDTH)
+            near_v = with_ones(near[1].reshape(2 * ROWS, WIDTH))
             for n in range(GROUP):
-                for p in (0, 1):
-                    x = q_other[p * SIDE : (p + 1) * SIDE, n * WIDTH : (n + 1) * WIDTH]
-                    qs_x[pl.ds(p * 512 + n * SIDE, SIDE), :] = x
-
-        @pl.when((t <= 1) | (t == 9))
+                tile(own, n * ROWS, near_k, near_v, allowed[n // 4])
+
+        @pl.when((t == 0) | (t == 2))
         def _():
             keys, values = unit(u)
             for n in range(GROUP):
                 tile(own, n * ROWS, keys, values)
 
-        @pl.when((t == 2) | (t == 3) | (t == 8))
+        @pl.when((t == 3) | (t == 4))
         def _():
             keys, values = unit(u)
             for n in range(GROUP):
                 tile(partner, n * ROWS, keys, values)
 
-        @pl.when((t >= 4) & (t <= 7))
+        @pl.when((t >= 5) & (t <= 9))
         def _():
             keys, values = unit(u)
             for n in range(GROUP):
@@ -260,34 +263,43 @@
                     part_out[part, pl.ds(n * ROWS, ROWS), :] = (refs[2][rows, :WIDTH] / total).astype(BF16)
                     lse = refs[1][rows, :] + jnp.log2(total)
                     lse_out[part, pl.ds(n, 1), :] = jnp.sum(jnp.where(eye, lse, 0.0), axis=0, keepdims=True)
-                send_part(part).start()
+                    if n % 2 == 1:
+                        send_part(part, n // 2).start()
                 send_lse(part).start()
+            spread_w(0).wait_recv()
+            mate_w(0).start()
             for n in range(4):
                 tile(own, xl * 512 + n * ROWS, keys, values)
 
-        @pl.when((t <= 1) | ((t >= 3) & (t <= 6)) | (t == 8))
-        def _():
-            after_it = jnp.where(t <= 1, t + 1, jnp.where(t == 8, 7, t))
-            pass_on(kv_at, ring_send, ring_recv, after_it)
-            to_mate(after_it, 0).start()
-            to_mate(after_it, 1).start()
-
-        @pl.when(t == 0)
+        @pl.when((t == 1) | (t == 2))
+        def _():
+            receive(t)
+
+        @pl.when(t == 1)
         def _():
             for k in (2, 1, 0):
                 spread_w(k).start()
             mate_w(3).start()
 
-        @pl.when(t == 6)
-        def _():
+        @pl.when(t == 2)
+        def _():
+            send_q.wait_recv()
+            for n in range(GROUP):
+                for p in (0, 1):
+                    x = q_other[p * SIDE : (p + 1) * SIDE, n * WIDTH : (n + 1) * WIDTH]
+                    qs_x[pl.ds(p * 512 + n * SIDE, SIDE), :] = x
+
+        @pl.when((t == 4) | (t == 6))
+        def _():
+            receive(t - 1)
+            receive(t)
+
+        @pl.when(t == 8)
+        def _():
+            receive(7)
             for k in (1, 2):
                 spread_w(k).wait_recv()
                 mate_w(k).start()
-
-        @pl.when(t == 9)
-        def _():
-            spread_w(0).wait_recv()
-            mate_w(0).start()
 
         return 0
 
@@ -306,7 +318,8 @@
         cb[0, piece, :, (2 * n + 1) * WIDTH : (2 * n + 2) * WIDTH] = mixed[SIDE:]
 
     def received(part):
-        send_part(part).wait_recv()
+        send_part(part, 0).wait_recv()
+        send_part(part, 1).wait_recv()
         send_lse(part).wait_recv()
 
     received(0)
@@ -331,16 +344,15 @@
         for n in range(1, 4):
             act((y + n) % 4)
 
-    def spread(k):
-        each_y(lambda there: partial_to(k, there).start())
-
     def alone(k, u):
-        for q in range(4):
+        for n in (2, 1, 3, 0):
+            q = (y + n) % 4
             value = jnp.dot(cb[u, 0], wg[0, q], preferred_element_type=F32)
             value = value + jnp.dot(cb[u, 1], wg[1, q], preferred_element_type=F32)
             ps[k, q, 0] = value.astype(BF16)
             ps[k, q, 1] = jnp.zeros((SIDE, 256), BF16)
-        spread(k)
+            if n:
+                partial_to(k, q).start()
 
     def to_z(k, d):
         there = (z + k * (2 * d - 1) + 8) % 8
@@ -383,6 +395,20 @@
         hand_over(zr.at[source], source)
 
     alone(0, 0)
+    all_sent(kv_at, ring_send, ring_recv)
+    for u in range(8):
+        for d in (0, 1):
+            to_mate(u, d).wait_send()
+    send_q.wait_send()
+    send_nk.wait_send()
+    send_nv.wait_send()
+    for k in range(3):
+        send_part(k, 0).wait_send()
+        send_part(k, 1).wait_send()
+        send_lse(k).wait_send()
+        spread_w(k).wait_send()
+    for k in range(4):
+        mate_w(k).wait_send()
 
     def stage(k, _):
         u = 2 * k - 1
@@ -392,10 +418,12 @@
             half_sum[q] = jnp.dot(rows, wg[0, q], preferred_element_type=F32)
         pass_on(cb_at, cb_send, cb_recv, u + 1)
         rows = cb[u + 1].reshape(ROWS, 1024)
-        for q in range(4):
+        for n in (2, 1, 3, 0):
+            q = (y + n) % 4
             value = (half_sum[q] + jnp.dot(rows, wg[1, q], preferred_element_type=F32)).astype(BF16)
             ps[k, q] = value.reshape(2, SIDE, 256)
-        spread(k)
+            if n:
+                partial_to(k, q).start()
 
         @pl.when(k >= 2)
         def _():
@@ -439,19 +467,6 @@
         if 0 < k < 4:
             to_z(k, 1).wait_send()
     all_sent(cb_at, cb_send, cb_recv)
-    all_sent(kv_at, ring_send, ring_recv)
-    for u in range(8):
-        for d in (0, 1):
-            to_mate(u, d).wait_send()
-    send_q.wait_send()
-    send_nk.wait_send()
-    send_nv.wait_send()
-    for k in range(3):
-        send_part(k).wait_send()
-        send_lse(k).wait_send()
-        spread_w(k).wait_send()
-    for k in range(4):
-        mate_w(k).wait_send()
 
 
 def on_device(q, k, v, rk, rv, seg, w):
@@ -490,7 +505,7 @@
             dma((2,)), dma((2,)),
             dma((2,)),
             dma((7,)), dma((7,)),
-            dma((3,)), dma((3,)),
+            dma((3, 2)), dma((3, 2)),
             dma((3,)), dma((3,)),
             dma((8, 2)), dma((8, 2)),
             dma((5, 4)), dma((5, 4)),

time: 93.6 us -> 91.5 us (0.978)
  Pallas kernels: 91 us -> 89.7 us
    pallas_call x1, Pallas kernels: 91 us -> 89.7 us  [on_device(): pl.pallas_call(whole, out_shape=jax.ShapeDtypeStruct((ROWS, 1024), BF16),...]
where the time goes in v3:
time: 91.5 us; the launch traced here: 91.4 us
  Pallas kernels  89.7 us (98%)
  local copies, waits for them, and re-layouts  1.67 us (2%)
    pallas_call x1, Pallas kernels, on_device(): pl.pallas_call(whole, out_shape=jax.ShapeDtypeStruct((ROWS, 1024), BF16),...  89.7 us

profile of v3, /device:TPU:16, one launch (start us, length us, event | category | flops | bytes accessed | tf_op | source)
XLA Modules:
  0.0 91.4 jit_solution(9074107244442732412)
XLA Ops:
  0.0 89.7 %shard_map.73 = bf16[128,1024]{1,0:T(8,128)(2,1)} custom-call(bf16[128,1024]{1,0:T(8,128)(2,1)} %q_hbm.1, bf16[512,128]{1,0:T(8,128)(2,1)} %k_hbm.1, bf16[512,128]{1,0:T(8,128)(2,1)} %v_hbm.1, bf16[128,128]{1,0:T(8,128)(2,1)} %rk_hbm.1, bf16[128,128]{1,0:T(8,128)(2,1)} %rv_hbm.1, s32[32,128]{1,0:T(8,128)} %bitcast.1, bf16[1024,256]{1,0:T(8,128)(2,1)} %w_hbm.1), custom_call_target="tpu_custom_call" | custom-call | tf_op jit(solution)/shard_map/pallas_call | solution.py:474
  89.7 1.7 %copy.9 = bf16[128,1024]{1,0:T(8,128)(2,1)} copy(bf16[128,1024]{1,0:T(8,128)(2,1)} %shard_map.73) | data formatting | bytes 524288

commit v4 on v3

--- a/solution.py
+++ b/solution.py
@@ -289,9 +289,8 @@
                     x = q_other[p * SIDE : (p + 1) * SIDE, n * WIDTH : (n + 1) * WIDTH]
                     qs_x[pl.ds(p * 512 + n * SIDE, SIDE), :] = x
 
-        @pl.when((t == 4) | (t == 6))
-        def _():
-            receive(t - 1)
+        @pl.when((t >= 3) & (t <= 6))
+        def _():
             receive(t)
 
         @pl.when(t == 8)
@@ -344,15 +343,29 @@
         for n in range(1, 4):
             act((y + n) % 4)
 
+    def block_alone(k, u, q):
+        value = jnp.dot(cb[u, 0], wg[0, q], preferred_element_type=F32)
+        value = value + jnp.dot(cb[u, 1], wg[1, q], preferred_element_type=F32)
+        ps[k, q, 0] = value.astype(BF16)
+        ps[k, q, 1] = jnp.zeros((SIDE, 256), BF16)
+
     def alone(k, u):
         for n in (2, 1, 3, 0):
             q = (y + n) % 4
-            value = jnp.dot(cb[u, 0], wg[0, q], preferred_element_type=F32)
-            value = value + jnp.dot(cb[u, 1], wg[1, q], preferred_element_type=F32)
-            ps[k, q, 0] = value.astype(BF16)
-            ps[k, q, 1] = jnp.zeros((SIDE, 256), BF16)
+            block_alone(k, u, q)
             if n:
                 partial_to(k, q).start()
+
+    def own_block(k, half):
+        @pl.when(k <= 2)
+        def _():
+            n = jnp.where(k == 1, 2 - half, 3 - 3 * half)
+            q = (y + n) % 4
+            block_alone(0, 0, q)
+
+            @pl.when(n > 0)
+            def _():
+                partial_to(0, q).start()
 
     def to_z(k, d):
         there = (z + k * (2 * d - 1) + 8) % 8
@@ -394,7 +407,6 @@
         waited(zr.at[source], z_recv.at[source])
         hand_over(zr.at[source], source)
 
-    alone(0, 0)
     all_sent(kv_at, ring_send, ring_recv)
     for u in range(8):
         for d in (0, 1):
@@ -416,6 +428,7 @@
         rows = cb[u].reshape(ROWS, 1024)
         for q in range(4):
             half_sum[q] = jnp.dot(rows, wg[0, q], preferred_element_type=F32)
+        own_block(k, 0)
         pass_on(cb_at, cb_send, cb_recv, u + 1)
         rows = cb[u + 1].reshape(ROWS, 1024)
         for n in (2, 1, 3, 0):
@@ -424,6 +437,7 @@
             ps[k, q] = value.reshape(2, SIDE, 256)
             if n:
                 partial_to(k, q).start()
+        own_block(k, 1)
 
         @pl.when(k >= 2)
         def _():

time: 91.5 us -> 91.1 us (level)
  no operation moved by 1% of the time
where the time goes in v4:
time: 91.1 us; the launch traced here: 91 us
  Pallas kernels  89.3 us (98%)
  local copies, waits for them, and re-layouts  1.67 us (2%)
    pallas_call x1, Pallas kernels, on_device(): pl.pallas_call(whole, out_shape=jax.ShapeDtypeStruct((ROWS, 1024), BF16),...  89.3 us

profile of v4, /device:TPU:16, one launch (start us, length us, event | category | flops | bytes accessed | tf_op | source)
XLA Modules:
  0.0 91.0 jit_solution(4003875093062546513)
XLA Ops:
  0.0 89.3 %shard_map.73 = bf16[128,1024]{1,0:T(8,128)(2,1)} custom-call(bf16[128,1024]{1,0:T(8,128)(2,1)} %q_hbm.1, bf16[512,128]{1,0:T(8,128)(2,1)} %k_hbm.1, bf16[512,128]{1,0:T(8,128)(2,1)} %v_hbm.1, bf16[128,128]{1,0:T(8,128)(2,1)} %rk_hbm.1, bf16[128,128]{1,0:T(8,128)(2,1)} %rv_hbm.1, s32[32,128]{1,0:T(8,128)} %bitcast.1, bf16[1024,256]{1,0:T(8,128)(2,1)} %w_hbm.1), custom_call_target="tpu_custom_call" | custom-call | tf_op jit(solution)/shard_map/pallas_call | solution.py:488
  89.3 1.7 %copy.9 = bf16[128,1024]{1,0:T(8,128)(2,1)} copy(bf16[128,1024]{1,0:T(8,128)(2,1)} %shard_map.73) | data formatting | bytes 524288

commit v5 on v4

--- a/solution.py
+++ b/solution.py
@@ -88,6 +88,9 @@
     partners += [((b + 4 * n) % 32, h) for n in range(1, 8)] + [(b, (h + n) % 8) for n in range(1, 8)]
     for device in partners:
         pl.semaphore_signal(barrier, inc=1, device_id=device, device_id_type=MESH)
+    for t_ref, a_ref in ((top, acc), (top_x, acc_x)):
+        t_ref[...] = jnp.full((HALF, WIDTH), -1e30, F32)
+        a_ref[...] = jnp.zeros((HALF, 2 * WIDTH), F32)
     pl.semaphore_wait(barrier, len(partners))
 
     def ring(buf, send, recv, u, d):
@@ -162,15 +165,12 @@
     begin(kv_at, ring_send, ring_recv, 1)
     to_mate(0, 0).start()
     to_mate(0, 1).start()
-    for copy in loads[4:]:
+    for copy in loads[4:8]:
         copy.wait()
 
     for n in range(GROUP):
         for p in (0, 1):
             qs[pl.ds(p * 512 + n * SIDE, SIDE), :] = q_ref[p * SIDE : (p + 1) * SIDE, n * WIDTH : (n + 1) * WIDTH]
-    for t_ref, a_ref in ((top, acc), (top_x, acc_x)):
-        t_ref[...] = jnp.full((HALF, WIDTH), -1e30, F32)
-        a_ref[...] = jnp.zeros((HALF, 2 * WIDTH), F32)
 
     own_ids = seg_ref[pl.ds(b, 1), :].astype(F32)
     before_ids = seg_ref[pl.ds(jnp.maximum(b - 1, 0), 1), :].astype(F32)
@@ -266,8 +266,6 @@
                     if n % 2 == 1:
                         send_part(part, n // 2).start()
                 send_lse(part).start()
-            spread_w(0).wait_recv()
-            mate_w(0).start()
             for n in range(4):
                 tile(own, xl * 512 + n * ROWS, keys, values)
 
@@ -277,6 +275,7 @@
 
         @pl.when(t == 1)
         def _():
+            loads[8].wait()
             for k in (2, 1, 0):
                 spread_w(k).start()
             mate_w(3).start()
@@ -327,6 +326,8 @@
         total = acc[rows, WIDTH:]
         mix(0, n, acc[rows, :WIDTH] / total, top[rows, :] + jnp.log2(total), 0)
     begin(cb_at, cb_send, cb_recv, 0)
+    spread_w(0).wait_recv()
+    mate_w(0).start()
     received(1)
     received(2)
     for n in range(4):
@@ -348,13 +349,6 @@
         value = value + jnp.dot(cb[u, 1], wg[1, q], preferred_element_type=F32)
         ps[k, q, 0] = value.astype(BF16)
         ps[k, q, 1] = jnp.zeros((SIDE, 256), BF16)
-
-    def alone(k, u):
-        for n in (2, 1, 3, 0):
-            q = (y + n) % 4
-            block_alone(k, u, q)
-            if n:
-                partial_to(k, q).start()
 
     def own_block(k, half):
         @pl.when(k <= 2)
@@ -453,8 +447,17 @@
     lax.fori_loop(1, 4, stage, 0)
     sum_up(0)
     hand_over(red.at[0, 0], z)
-    pass_on(cb_at, cb_send, cb_recv, 7)
-    alone(4, 7)
+    waited(cb_at(7, 0), cb_recv.at[7, 0])
+    for q in range(4):
+        half_sum[q, :SIDE] = jnp.dot(cb[7, 0], wg[0, q], preferred_element_type=F32)
+    waited(cb_at(7, 1), cb_recv.at[7, 1])
+    for n in (2, 1, 3, 0):
+        q = (y + n) % 4
+        value = half_sum[q, :SIDE] + jnp.dot(cb[7, 1], wg[1, q], preferred_element_type=F32)
+        ps[4, q, 0] = value.astype(BF16)
+        ps[4, q, 1] = jnp.zeros((SIDE, 256), BF16)
+        if n:
+            partial_to(4, q).start()
     sum_up(3)
     deliver(2, 0)
     deliver(2, 1)

time: 91.1 us -> 91 us (level)
  no operation moved by 1% of the time
where the time goes in v5:
time: 91 us; the launch traced here: 90.9 us
  Pallas kernels  89.2 us (98%)
  local copies, waits for them, and re-layouts  1.67 us (2%)
    pallas_call x1, Pallas kernels, on_device(): pl.pallas_call(whole, out_shape=jax.ShapeDtypeStruct((ROWS, 1024), BF16),...  89.2 us

profile of v5, /device:TPU:16, one launch (start us, length us, event | category | flops | bytes accessed | tf_op | source)
XLA Modules:
  0.0 90.9 jit_solution(11206348233214242266)
XLA Ops:
  0.0 89.2 %shard_map.73 = bf16[128,1024]{1,0:T(8,128)(2,1)} custom-call(bf16[128,1024]{1,0:T(8,128)(2,1)} %q_hbm.1, bf16[512,128]{1,0:T(8,128)(2,1)} %k_hbm.1, bf16[512,128]{1,0:T(8,128)(2,1)} %v_hbm.1, bf16[128,128]{1,0:T(8,128)(2,1)} %rk_hbm.1, bf16[128,128]{1,0:T(8,128)(2,1)} %rv_hbm.1, s32[32,128]{1,0:T(8,128)} %bitcast.1, bf16[1024,256]{1,0:T(8,128)(2,1)} %w_hbm.1), custom_call_target="tpu_custom_call" | custom-call | tf_op jit(solution)/shard_map/pallas_call | solution.py:491
  89.2 1.7 %copy.9 = bf16[128,1024]{1,0:T(8,128)(2,1)} copy(bf16[128,1024]{1,0:T(8,128)(2,1)} %shard_map.73) | data formatting | bytes 524288

commit v6 on v5

--- a/solution.py
+++ b/solution.py
@@ -295,9 +295,6 @@
         @pl.when(t == 8)
         def _():
             receive(7)
-            for k in (1, 2):
-                spread_w(k).wait_recv()
-                mate_w(k).start()
 
         return 0
 
@@ -326,8 +323,9 @@
         total = acc[rows, WIDTH:]
         mix(0, n, acc[rows, :WIDTH] / total, top[rows, :] + jnp.log2(total), 0)
     begin(cb_at, cb_send, cb_recv, 0)
-    spread_w(0).wait_recv()
-    mate_w(0).start()
+    for k in range(3):
+        spread_w(k).wait_recv()
+        mate_w(k).start()
     received(1)
     received(2)
     for n in range(4):

time: 91 us -> 91 us (level)
  no operation moved by 1% of the time
where the time goes in v6:
time: 91 us; the launch traced here: 90.9 us
  Pallas kernels  89.3 us (98%)
  local copies, waits for them, and re-layouts  1.67 us (2%)
    pallas_call x1, Pallas kernels, on_device(): pl.pallas_call(whole, out_shape=jax.ShapeDtypeStruct((ROWS, 1024), BF16),...  89.3 us

profile of v6, /device:TPU:16, one launch (start us, length us, event | category | flops | bytes accessed | tf_op | source)
XLA Modules:
  0.0 90.9 jit_solution(13813761762087637261)
XLA Ops:
  0.0 89.3 %shard_map.73 = bf16[128,1024]{1,0:T(8,128)(2,1)} custom-call(bf16[128,1024]{1,0:T(8,128)(2,1)} %q_hbm.1, bf16[512,128]{1,0:T(8,128)(2,1)} %k_hbm.1, bf16[512,128]{1,0:T(8,128)(2,1)} %v_hbm.1, bf16[128,128]{1,0:T(8,128)(2,1)} %rk_hbm.1, bf16[128,128]{1,0:T(8,128)(2,1)} %rv_hbm.1, s32[32,128]{1,0:T(8,128)} %bitcast.1, bf16[1024,256]{1,0:T(8,128)(2,1)} %w_hbm.1), custom_call_target="tpu_custom_call" | custom-call | tf_op jit(solution)/shard_map/pallas_call | solution.py:489
  89.3 1.7 %copy.9 = bf16[128,1024]{1,0:T(8,128)(2,1)} copy(bf16[128,1024]{1,0:T(8,128)(2,1)} %shard_map.73) | data formatting | bytes 524288
